TPU v7x, 256 devices: a whole 4x4x8 slice. The times are simulated.
256 devices in a mesh: loop: 64 (over x_lo, z, y), team: 4 (over x_hi, core).
Axes of the slice: x: 4 (x_hi: 2, x_lo: 2; x = x_hi * 2 + x_lo), y: 4, z: 8, core: 2. Of those that a mesh axis runs over, the one named last changes fastest.
Arguments:
- samples: bfloat16 [4096, 11776], P(('loop', 'team')), may hold values from -6 to 6
- input_gains: float32 [2, 4096, 4, 128], P(None, 'loop', None, 'team'), may hold values from -5 to 5
Outputs:
- visibility: float32 [64, 4, 2, 256, 4096], P('loop', 'team')
All inputs are finite; a program needn't handle non-finite values.
Results may differ from a plain program's by a relative error of at most 0.0038.
Values may be sent and summed in bfloat16 or wider, within the bound.
No kernel may reach another device: no remote copies, remote signals or barrier semaphores. Data moves between devices by JAX's collectives and lax.ppermute only.
A program may use at most 64 MiB of HBM per device.

v0:
```python
import math
import jax
import jax.numpy as jnp
from jax import lax
from jax.sharding import PartitionSpec as P

FCH = 512
TAPS = 8
AVG = 32
SPEC = 16


def shifted(array, axis, by):
    count = lax.axis_size(axis)
    pairs = [(i, i + by) for i in range(count) if 0 <= i + by < count]
    return lax.ppermute(array, axis, pairs)


def from_behind(block, axis, distance):
    devices = range(lax.axis_size(axis))
    route = [((i - distance) % len(devices), i) for i in devices]
    return lax.ppermute(block, axis, route)


def pfb_window():
    sample_pos = jnp.arange(TAPS * FCH, dtype=jnp.float32) + 0.5
    taper = jnp.sin(jnp.pi * sample_pos / (TAPS * FCH)) ** 2
    taps_table = jnp.sinc(sample_pos / FCH - TAPS / 2) * taper
    return taps_table.reshape(TAPS, FCH)


def filter_bank(raw_rows, channel_index):
    rows_here = raw_rows.shape[0]
    frames = raw_rows.astype(jnp.float32).reshape(rows_here, SPEC + TAPS - 1, FCH)
    window = pfb_window()
    filtered = window[0] * frames[:, 0:SPEC, :]
    for tap_index in range(1, TAPS):
        filtered = filtered + window[tap_index] * frames[:, tap_index : tap_index + SPEC, :]
    channel_flat = channel_index.reshape(channel_index.shape[0], -1)
    positions = jnp.arange(FCH, dtype=jnp.int32)
    angles_table = (positions[:, None, None] * channel_flat[None] % FCH).astype(jnp.float32) * (
        2.0 * math.pi / FCH
    )
    dft_table = jnp.concatenate(
        [jnp.cos(angles_table), -jnp.sin(angles_table)], axis=2
    ) / math.sqrt(FCH)
    return jnp.einsum(
        "itp,pmc->imtc",
        filtered,
        dft_table,
        precision=lax.Precision.HIGHEST,
        preferred_element_type=jnp.float32,
    )


def apply_gains(spectra, gain_rows):
    rows_here = spectra.shape[0]
    bin_groups = gain_rows.shape[2]
    shaped = spectra.reshape(rows_here, SPEC, 2, bin_groups, AVG)
    real_part = shaped[:, :, 0]
    imag_part = shaped[:, :, 1]
    gain_re = gain_rows[0][:, None]
    gain_im = gain_rows[1][:, None]
    volt_re = (gain_re * real_part - gain_im * imag_part).astype(jnp.bfloat16)
    volt_im = (gain_re * imag_part + gain_im * real_part).astype(jnp.bfloat16)
    stacked = jnp.stack([volt_re, volt_im], axis=1)
    return stacked.transpose(3, 0, 1, 2, 4).reshape(bin_groups, rows_here, 2 * SPEC * AVG)


def local(samples, input_gains):
    member = lax.axis_index("team")
    team_size = lax.axis_size("team")
    loop_size = lax.axis_size("loop")
    loop_place = lax.axis_index("loop")
    team_rows = input_gains.shape[1]
    bin_groups = input_gains.shape[2]
    group_count = loop_size // bin_groups
    bin_slot = loop_place % bin_groups
    row_group = loop_place // bin_groups
    bin_range = jnp.arange(bin_groups, dtype=jnp.int32)
    avg_range = jnp.arange(AVG, dtype=jnp.int32)
    own_channels = (bin_range[:, None] * team_size + member) * AVG + avg_range[None, :]
    spectra = filter_bank(lax.all_gather(samples, "team", axis=0, tiled=True), own_channels[None])[
        :, 0
    ]
    packed_all = apply_gains(spectra, input_gains)
    width_k = packed_all.shape[2]
    own_part = lax.dynamic_index_in_dim(packed_all, bin_slot, 0, keepdims=False)
    gathered = jnp.zeros((bin_groups, team_rows, width_k), jnp.bfloat16)
    gathered = lax.dynamic_update_index_in_dim(gathered, own_part, bin_slot, 0)
    offsets = [value for value in range(1 - bin_groups, bin_groups) if value != 0]
    for row_offset in offsets:
        send_slot = jnp.clip(bin_slot + row_offset, 0, bin_groups - 1)
        outgoing = lax.dynamic_index_in_dim(packed_all, send_slot, 0, keepdims=False)
        incoming = shifted(outgoing, "loop", row_offset)
        anchor_slot = bin_slot - row_offset
        from_group = (anchor_slot >= 0) & (anchor_slot < bin_groups)
        store_slot = jnp.clip(anchor_slot, 0, bin_groups - 1)
        kept_rows = lax.dynamic_index_in_dim(gathered, store_slot, 0, keepdims=False)
        gathered = lax.dynamic_update_index_in_dim(
            gathered, jnp.where(from_group, incoming, kept_rows), store_slot, 0
        )
    rows_block = gathered.reshape(bin_groups * team_rows, width_k)
    width_rows = rows_block.shape[0]
    half_width = width_k // 2
    rotated = jnp.concatenate([rows_block[:, half_width:], -rows_block[:, :half_width]], axis=1)
    local_pair = jnp.stack([rows_block, rotated])
    norm_scale = 1.0 / (AVG * SPEC)
    nought = jnp.zeros((), jnp.int32)

    def place_tile(tile_state, partner, source_group):
        tile_values = (
            jnp.einsum("crk,pk->crp", local_pair, partner, preferred_element_type=jnp.float32)
            * norm_scale
        )
        start_col = source_group * width_rows
        return lax.dynamic_update_slice(tile_state, tile_values, (nought, nought, start_col))

    visibility = jnp.zeros((2, width_rows, width_rows * group_count), jnp.float32)
    visibility = place_tile(visibility, rows_block, row_group)

    def visit(visit_index, carry):
        partner, tile_state = carry
        partner = from_behind(partner, "loop", bin_groups)
        return (partner, place_tile(tile_state, partner, (row_group - visit_index) % group_count))

    partner, visibility = lax.fori_loop(1, group_count, visit, (rows_block, visibility))
    return visibility[None, None]


def solution(mesh):
    placed = (P(("loop", "team"), None), P(None, "loop", None, "team"))
    return jax.shard_map(
        local,
        mesh=mesh,
        in_specs=placed,
        out_specs=P("loop", "team", None, None, None),
        check_vma=False,
    )
```

profile of v0, /device:TPU:26, one launch (start us, length us, event | category | flops | bytes accessed | tf_op | source)
XLA Modules:
  0.0 318.6 jit_solution(12989422514897380619)
XLA Ops:
  6.5 0.7 all-gather.2.cloned.1.call-update
  8.2 0.9 slice_bitcast_fusion.3
  9.1 1.8 fusion.26
  10.9 26.0 %all-gather.2.cloned.1.call-done = bf16[64,11776]{1,0:T(8,128)(2,1)} async-done(((bf16[16,11776]{1,0:T(8,128)(2,1)}), bf16[64,11776]{1,0:T(8,128)(2,1)}) %all-gather.2.cloned.1.call-update) | async-done | bytes 1507344 | tf_op jit(solution)/shard_map/all_gather | solution.py:83
  36.9 2.7 reshape.165
  39.6 2.8 fusion.2
  42.3 2.7 fusion.11
  47.4 2.4 collective-permute-start.1
  49.8 8.0 %collective-permute-start.2 = (bf16[64,1024]{1,0:T(8,128)(2,1)S(1)}, bf16[64,1024]{1,0:T(8,128)(2,1)S(1)}, u32[]{:S(2)}, u32[]{:S(2)}) collective-permute-start(bf16[64,1024]{1,0:T(8,128)(2,1)S(1)} %bitcast.98), channel_id=1, source_target_pairs={{8,0},{12,4},{16,8},{20,12},{24,16},{28,20},{32,24},{36,28},{40,32... | collective-permute-start | bytes 393224 | tf_op jit(solution)/shard_map/ppermute | solution.py:16
  57.8 1.9 collective-permute-start.3
  59.7 6.0 %collective-permute-start.4 = (bf16[64,1024]{1,0:T(8,128)(2,1)S(1)}, bf16[64,1024]{1,0:T(8,128)(2,1)S(1)}, u32[]{:S(2)}, u32[]{:S(2)}) collective-permute-start(bf16[64,1024]{1,0:T(8,128)(2,1)S(1)} %bitcast.96), channel_id=1, source_target_pairs={{0,4},{4,8},{8,12},{12,16},{16,20},{20,24},{24,28},{28,32},{32,36}... | collective-permute-start | bytes 393224 | tf_op jit(solution)/shard_map/ppermute | solution.py:16
  65.9 1.9 collective-permute-start.5
  67.9 1.9 collective-permute-start.6
  70.1 4.3 %collective-permute-done.5 = bf16[64,1024]{1,0:T(8,128)(2,1)S(1)} collective-permute-done((bf16[64,1024]{1,0:T(8,128)(2,1)S(1)}, bf16[64,1024]{1,0:T(8,128)(2,1)S(1)}, u32[]{:S(2)}, u32[]{:S(2)}) %collective-permute-start.5) | collective-permute-done | bytes 131104 | tf_op jit(solution)/shard_map/ppermute | solution.py:16
  74.4 2.5 collective-permute-done.6
  77.2 1.0 broadcast_in_dim.44
  78.7 3.4 %copy-done = f32[2,256,4096]{2,1,0:T(8,128)} copy-done((f32[2,256,4096]{2,1,0:T(8,128)}, f32[2,256,4096]{2,1,0:T(8,128)S(1)}, u32[]{:S(2)}) %copy-start) | copy-done | bytes 8388632
  82.1 229.7 %while.17 = (s32[]{:T(128)}, bf16[256,1024]{1,0:T(8,128)(2,1)S(1)}, f32[2,256,4096]{2,1,0:T(8,128)}, bf16[2,256,1024]{2,1,0:T(8,128)(2,1)S(1)}, s32[]{:T(128)}, ...) while((s32[]{:T(128)}, bf16[256,1024]{1,0:T(8,128)(2,1)S(1)}, ...), condition=%wide.region_1.2_spmd, body=%wide.region_0.1_spmd.sunk | while | flops 268566560 | bytes 5243200 | solution.py:127
  82.1 15.5 %collective-permute-done = bf16[256,1024]{1,0:T(8,128)(2,1)S(1)} collective-permute-done((bf16[256,1024]{1,0:T(8,128)(2,1)S(1)}, bf16[256,1024]{1,0:T(8,128)(2,1)S(1)}, u32[]{:S(2)}, u32[]{:S(2)}) %collective-permute-start) | collective-permute-done | bytes 524320 | tf_op jit(solution)/shard_map/while/body/eval_jaxpr/ppermute | solution.py:22
  97.7 1.3 fusion.51
  98.9 14.6 %collective-permute-done = bf16[256,1024]{1,0:T(8,128)(2,1)S(1)} collective-permute-done((bf16[256,1024]{1,0:T(8,128)(2,1)S(1)}, bf16[256,1024]{1,0:T(8,128)(2,1)S(1)}, u32[]{:S(2)}, u32[]{:S(2)}) %collective-permute-start) | collective-permute-done | bytes 524320 | tf_op jit(solution)/shard_map/while/body/eval_jaxpr/ppermute | solution.py:22
  113.5 1.3 fusion.51
  114.8 13.7 %collective-permute-done = bf16[256,1024]{1,0:T(8,128)(2,1)S(1)} collective-permute-done((bf16[256,1024]{1,0:T(8,128)(2,1)S(1)}, bf16[256,1024]{1,0:T(8,128)(2,1)S(1)}, u32[]{:S(2)}, u32[]{:S(2)}) %collective-permute-start) | collective-permute-done | bytes 524320 | tf_op jit(solution)/shard_map/while/body/eval_jaxpr/ppermute | solution.py:22
  128.5 1.3 fusion.51
  129.8 12.7 %collective-permute-done = bf16[256,1024]{1,0:T(8,128)(2,1)S(1)} collective-permute-done((bf16[256,1024]{1,0:T(8,128)(2,1)S(1)}, bf16[256,1024]{1,0:T(8,128)(2,1)S(1)}, u32[]{:S(2)}, u32[]{:S(2)}) %collective-permute-start) | collective-permute-done | bytes 524320 | tf_op jit(solution)/shard_map/while/body/eval_jaxpr/ppermute | solution.py:22
  142.6 1.3 fusion.51
  143.9 11.8 %collective-permute-done = bf16[256,1024]{1,0:T(8,128)(2,1)S(1)} collective-permute-done((bf16[256,1024]{1,0:T(8,128)(2,1)S(1)}, bf16[256,1024]{1,0:T(8,128)(2,1)S(1)}, u32[]{:S(2)}, u32[]{:S(2)}) %collective-permute-start) | collective-permute-done | bytes 524320 | tf_op jit(solution)/shard_map/while/body/eval_jaxpr/ppermute | solution.py:22
  155.7 1.3 fusion.51
  157.0 11.4 %collective-permute-done = bf16[256,1024]{1,0:T(8,128)(2,1)S(1)} collective-permute-done((bf16[256,1024]{1,0:T(8,128)(2,1)S(1)}, bf16[256,1024]{1,0:T(8,128)(2,1)S(1)}, u32[]{:S(2)}, u32[]{:S(2)}) %collective-permute-start) | collective-permute-done | bytes 524320 | tf_op jit(solution)/shard_map/while/body/eval_jaxpr/ppermute | solution.py:22
  168.4 1.3 fusion.51
  169.7 12.5 %collective-permute-done = bf16[256,1024]{1,0:T(8,128)(2,1)S(1)} collective-permute-done((bf16[256,1024]{1,0:T(8,128)(2,1)S(1)}, bf16[256,1024]{1,0:T(8,128)(2,1)S(1)}, u32[]{:S(2)}, u32[]{:S(2)}) %collective-permute-start) | collective-permute-done | bytes 524320 | tf_op jit(solution)/shard_map/while/body/eval_jaxpr/ppermute | solution.py:22
  182.2 1.3 fusion.51
  183.5 13.6 %collective-permute-done = bf16[256,1024]{1,0:T(8,128)(2,1)S(1)} collective-permute-done((bf16[256,1024]{1,0:T(8,128)(2,1)S(1)}, bf16[256,1024]{1,0:T(8,128)(2,1)S(1)}, u32[]{:S(2)}, u32[]{:S(2)}) %collective-permute-start) | collective-permute-done | bytes 524320 | tf_op jit(solution)/shard_map/while/body/eval_jaxpr/ppermute | solution.py:22
  197.1 1.3 fusion.51
  198.4 14.6 %collective-permute-done = bf16[256,1024]{1,0:T(8,128)(2,1)S(1)} collective-permute-done((bf16[256,1024]{1,0:T(8,128)(2,1)S(1)}, bf16[256,1024]{1,0:T(8,128)(2,1)S(1)}, u32[]{:S(2)}, u32[]{:S(2)}) %collective-permute-start) | collective-permute-done | bytes 524320 | tf_op jit(solution)/shard_map/while/body/eval_jaxpr/ppermute | solution.py:22
  213.0 1.3 fusion.51
  214.3 15.8 %collective-permute-done = bf16[256,1024]{1,0:T(8,128)(2,1)S(1)} collective-permute-done((bf16[256,1024]{1,0:T(8,128)(2,1)S(1)}, bf16[256,1024]{1,0:T(8,128)(2,1)S(1)}, u32[]{:S(2)}, u32[]{:S(2)}) %collective-permute-start) | collective-permute-done | bytes 524320 | tf_op jit(solution)/shard_map/while/body/eval_jaxpr/ppermute | solution.py:22
  230.1 1.3 fusion.51
  231.4 16.9 %collective-permute-done = bf16[256,1024]{1,0:T(8,128)(2,1)S(1)} collective-permute-done((bf16[256,1024]{1,0:T(8,128)(2,1)S(1)}, bf16[256,1024]{1,0:T(8,128)(2,1)S(1)}, u32[]{:S(2)}, u32[]{:S(2)}) %collective-permute-start) | collective-permute-done | bytes 524320 | tf_op jit(solution)/shard_map/while/body/eval_jaxpr/ppermute | solution.py:22
  248.3 1.3 fusion.51
  249.6 16.0 %collective-permute-done = bf16[256,1024]{1,0:T(8,128)(2,1)S(1)} collective-permute-done((bf16[256,1024]{1,0:T(8,128)(2,1)S(1)}, bf16[256,1024]{1,0:T(8,128)(2,1)S(1)}, u32[]{:S(2)}, u32[]{:S(2)}) %collective-permute-start) | collective-permute-done | bytes 524320 | tf_op jit(solution)/shard_map/while/body/eval_jaxpr/ppermute | solution.py:22
  265.7 1.3 fusion.51
  267.0 15.2 %collective-permute-done = bf16[256,1024]{1,0:T(8,128)(2,1)S(1)} collective-permute-done((bf16[256,1024]{1,0:T(8,128)(2,1)S(1)}, bf16[256,1024]{1,0:T(8,128)(2,1)S(1)}, u32[]{:S(2)}, u32[]{:S(2)}) %collective-permute-start) | collective-permute-done | bytes 524320 | tf_op jit(solution)/shard_map/while/body/eval_jaxpr/ppermute | solution.py:22
  282.2 1.3 fusion.51
  283.5 14.3 %collective-permute-done = bf16[256,1024]{1,0:T(8,128)(2,1)S(1)} collective-permute-done((bf16[256,1024]{1,0:T(8,128)(2,1)S(1)}, bf16[256,1024]{1,0:T(8,128)(2,1)S(1)}, u32[]{:S(2)}, u32[]{:S(2)}) %collective-permute-start) | collective-permute-done | bytes 524320 | tf_op jit(solution)/shard_map/while/body/eval_jaxpr/ppermute | solution.py:22
  297.9 1.3 fusion.51
  299.1 11.3 %collective-permute-done = bf16[256,1024]{1,0:T(8,128)(2,1)S(1)} collective-permute-done((bf16[256,1024]{1,0:T(8,128)(2,1)S(1)}, bf16[256,1024]{1,0:T(8,128)(2,1)S(1)}, u32[]{:S(2)}, u32[]{:S(2)}) %collective-permute-start) | collective-permute-done | bytes 524320 | tf_op jit(solution)/shard_map/while/body/eval_jaxpr/ppermute | solution.py:22
  310.5 1.3 fusion.51
  (73 shorter events, 4.8 us)
Async XLA Ops:
  6.5 30.3 %all-gather.2.cloned.1.call-start = ((), (), s32[]{:S(2)}) async-start(), calls=%async_computation | async-start | bytes 1884160 | tf_op jit(solution)/shard_map/all_gather | solution.py:83
  39.5 2.8 copy-start.1
  47.4 20.4 %collective-permute-start.1 = (bf16[64,1024]{1,0:T(8,128)(2,1)S(1)}, bf16[64,1024]{1,0:T(8,128)(2,1)S(1)}, u32[]{:S(2)}, u32[]{:S(2)}) collective-permute-start(bf16[64,1024]{1,0:T(8,128)(2,1)S(1)} %bitcast.99), channel_id=1, source_target_pairs={{12,0},{16,4},{20,8},{24,12},{28,16},{32,20},{36,24},{40,28},{44,3... | collective-permute-start | bytes 393224 | tf_op jit(solution)/shard_map/ppermute | solution.py:16
  49.8 20.0 %collective-permute-start.2 = (bf16[64,1024]{1,0:T(8,128)(2,1)S(1)}, bf16[64,1024]{1,0:T(8,128)(2,1)S(1)}, u32[]{:S(2)}, u32[]{:S(2)}) collective-permute-start(bf16[64,1024]{1,0:T(8,128)(2,1)S(1)} %bitcast.98), channel_id=1, source_target_pairs={{8,0},{12,4},{16,8},{20,12},{24,16},{28,20},{32,24},{36,28},{40,32... | collective-permute-start | bytes 393224 | tf_op jit(solution)/shard_map/ppermute | solution.py:16
  57.8 12.1 %collective-permute-start.3 = (bf16[64,1024]{1,0:T(8,128)(2,1)S(1)}, bf16[64,1024]{1,0:T(8,128)(2,1)S(1)}, u32[]{:S(2)}, u32[]{:S(2)}) collective-permute-start(bf16[64,1024]{1,0:T(8,128)(2,1)S(1)} %bitcast.97), channel_id=1, source_target_pairs={{4,0},{8,4},{12,8},{16,12},{20,16},{24,20},{28,24},{32,28},{36,32}... | collective-permute-start | bytes 393224 | tf_op jit(solution)/shard_map/ppermute | solution.py:16
  59.7 10.3 %collective-permute-start.4 = (bf16[64,1024]{1,0:T(8,128)(2,1)S(1)}, bf16[64,1024]{1,0:T(8,128)(2,1)S(1)}, u32[]{:S(2)}, u32[]{:S(2)}) collective-permute-start(bf16[64,1024]{1,0:T(8,128)(2,1)S(1)} %bitcast.96), channel_id=1, source_target_pairs={{0,4},{4,8},{8,12},{12,16},{16,20},{20,24},{24,28},{28,32},{32,36}... | collective-permute-start | bytes 393224 | tf_op jit(solution)/shard_map/ppermute | solution.py:16
  65.9 8.5 %collective-permute-start.5 = (bf16[64,1024]{1,0:T(8,128)(2,1)S(1)}, bf16[64,1024]{1,0:T(8,128)(2,1)S(1)}, u32[]{:S(2)}, u32[]{:S(2)}) collective-permute-start(bf16[64,1024]{1,0:T(8,128)(2,1)S(1)} %bitcast.95), channel_id=1, source_target_pairs={{0,8},{4,12},{8,16},{12,20},{16,24},{20,28},{24,32},{28,36},{32,40... | collective-permute-start | bytes 393224 | tf_op jit(solution)/shard_map/ppermute | solution.py:16
  67.9 9.0 %collective-permute-start.6 = (bf16[64,1024]{1,0:T(8,128)(2,1)S(1)}, bf16[64,1024]{1,0:T(8,128)(2,1)S(1)}, u32[]{:S(2)}, u32[]{:S(2)}) collective-permute-start(bf16[64,1024]{1,0:T(8,128)(2,1)S(1)} %bitcast.94), channel_id=1, source_target_pairs={{0,12},{4,16},{8,20},{12,24},{16,28},{20,32},{24,36},{28,40},{32,4... | collective-permute-start | bytes 393224 | tf_op jit(solution)/shard_map/ppermute | solution.py:16
  78.7 3.4 %copy-start = (f32[2,256,4096]{2,1,0:T(8,128)}, f32[2,256,4096]{2,1,0:T(8,128)S(1)}, u32[]{:S(2)}) copy-start(f32[2,256,4096]{2,1,0:T(8,128)S(1)} %fusion.14) | copy-start | bytes 25165828
  82.1 15.5 %collective-permute-start = (bf16[256,1024]{1,0:T(8,128)(2,1)S(1)}, bf16[256,1024]{1,0:T(8,128)(2,1)S(1)}, u32[]{:S(2)}, u32[]{:S(2)}) collective-permute-start(bf16[256,1024]{1,0:T(8,128)(2,1)S(1)} %get-tuple-element.215), channel_id=1, source_target_pairs={{240,0},{244,4},{248,8},{252,12},{0,16},{4,20},{8,24},{12,28},{16,... | collective-permute-start | bytes 1572872 | tf_op jit(solution)/shard_map/while/body/eval_jaxpr/ppermute | solution.py:22
  98.9 14.6 %collective-permute-start = (bf16[256,1024]{1,0:T(8,128)(2,1)S(1)}, bf16[256,1024]{1,0:T(8,128)(2,1)S(1)}, u32[]{:S(2)}, u32[]{:S(2)}) collective-permute-start(bf16[256,1024]{1,0:T(8,128)(2,1)S(1)} %get-tuple-element.215), channel_id=1, source_target_pairs={{240,0},{244,4},{248,8},{252,12},{0,16},{4,20},{8,24},{12,28},{16,... | collective-permute-start | bytes 1572872 | tf_op jit(solution)/shard_map/while/body/eval_jaxpr/ppermute | solution.py:22
  114.8 13.7 %collective-permute-start = (bf16[256,1024]{1,0:T(8,128)(2,1)S(1)}, bf16[256,1024]{1,0:T(8,128)(2,1)S(1)}, u32[]{:S(2)}, u32[]{:S(2)}) collective-permute-start(bf16[256,1024]{1,0:T(8,128)(2,1)S(1)} %get-tuple-element.215), channel_id=1, source_target_pairs={{240,0},{244,4},{248,8},{252,12},{0,16},{4,20},{8,24},{12,28},{16,... | collective-permute-start | bytes 1572872 | tf_op jit(solution)/shard_map/while/body/eval_jaxpr/ppermute | solution.py:22
  129.8 12.7 %collective-permute-start = (bf16[256,1024]{1,0:T(8,128)(2,1)S(1)}, bf16[256,1024]{1,0:T(8,128)(2,1)S(1)}, u32[]{:S(2)}, u32[]{:S(2)}) collective-permute-start(bf16[256,1024]{1,0:T(8,128)(2,1)S(1)} %get-tuple-element.215), channel_id=1, source_target_pairs={{240,0},{244,4},{248,8},{252,12},{0,16},{4,20},{8,24},{12,28},{16,... | collective-permute-start | bytes 1572872 | tf_op jit(solution)/shard_map/while/body/eval_jaxpr/ppermute | solution.py:22
  143.9 11.8 %collective-permute-start = (bf16[256,1024]{1,0:T(8,128)(2,1)S(1)}, bf16[256,1024]{1,0:T(8,128)(2,1)S(1)}, u32[]{:S(2)}, u32[]{:S(2)}) collective-permute-start(bf16[256,1024]{1,0:T(8,128)(2,1)S(1)} %get-tuple-element.215), channel_id=1, source_target_pairs={{240,0},{244,4},{248,8},{252,12},{0,16},{4,20},{8,24},{12,28},{16,... | collective-permute-start | bytes 1572872 | tf_op jit(solution)/shard_map/while/body/eval_jaxpr/ppermute | solution.py:22
  157.0 11.4 %collective-permute-start = (bf16[256,1024]{1,0:T(8,128)(2,1)S(1)}, bf16[256,1024]{1,0:T(8,128)(2,1)S(1)}, u32[]{:S(2)}, u32[]{:S(2)}) collective-permute-start(bf16[256,1024]{1,0:T(8,128)(2,1)S(1)} %get-tuple-element.215), channel_id=1, source_target_pairs={{240,0},{244,4},{248,8},{252,12},{0,16},{4,20},{8,24},{12,28},{16,... | collective-permute-start | bytes 1572872 | tf_op jit(solution)/shard_map/while/body/eval_jaxpr/ppermute | solution.py:22
  169.7 12.5 %collective-permute-start = (bf16[256,1024]{1,0:T(8,128)(2,1)S(1)}, bf16[256,1024]{1,0:T(8,128)(2,1)S(1)}, u32[]{:S(2)}, u32[]{:S(2)}) collective-permute-start(bf16[256,1024]{1,0:T(8,128)(2,1)S(1)} %get-tuple-element.215), channel_id=1, source_target_pairs={{240,0},{244,4},{248,8},{252,12},{0,16},{4,20},{8,24},{12,28},{16,... | collective-permute-start | bytes 1572872 | tf_op jit(solution)/shard_map/while/body/eval_jaxpr/ppermute | solution.py:22
  183.5 13.6 %collective-permute-start = (bf16[256,1024]{1,0:T(8,128)(2,1)S(1)}, bf16[256,1024]{1,0:T(8,128)(2,1)S(1)}, u32[]{:S(2)}, u32[]{:S(2)}) collective-permute-start(bf16[256,1024]{1,0:T(8,128)(2,1)S(1)} %get-tuple-element.215), channel_id=1, source_target_pairs={{240,0},{244,4},{248,8},{252,12},{0,16},{4,20},{8,24},{12,28},{16,... | collective-permute-start | bytes 1572872 | tf_op jit(solution)/shard_map/while/body/eval_jaxpr/ppermute | solution.py:22
  198.4 14.6 %collective-permute-start = (bf16[256,1024]{1,0:T(8,128)(2,1)S(1)}, bf16[256,1024]{1,0:T(8,128)(2,1)S(1)}, u32[]{:S(2)}, u32[]{:S(2)}) collective-permute-start(bf16[256,1024]{1,0:T(8,128)(2,1)S(1)} %get-tuple-element.215), channel_id=1, source_target_pairs={{240,0},{244,4},{248,8},{252,12},{0,16},{4,20},{8,24},{12,28},{16,... | collective-permute-start | bytes 1572872 | tf_op jit(solution)/shard_map/while/body/eval_jaxpr/ppermute | solution.py:22
  214.3 15.8 %collective-permute-start = (bf16[256,1024]{1,0:T(8,128)(2,1)S(1)}, bf16[256,1024]{1,0:T(8,128)(2,1)S(1)}, u32[]{:S(2)}, u32[]{:S(2)}) collective-permute-start(bf16[256,1024]{1,0:T(8,128)(2,1)S(1)} %get-tuple-element.215), channel_id=1, source_target_pairs={{240,0},{244,4},{248,8},{252,12},{0,16},{4,20},{8,24},{12,28},{16,... | collective-permute-start | bytes 1572872 | tf_op jit(solution)/shard_map/while/body/eval_jaxpr/ppermute | solution.py:22
  231.4 16.9 %collective-permute-start = (bf16[256,1024]{1,0:T(8,128)(2,1)S(1)}, bf16[256,1024]{1,0:T(8,128)(2,1)S(1)}, u32[]{:S(2)}, u32[]{:S(2)}) collective-permute-start(bf16[256,1024]{1,0:T(8,128)(2,1)S(1)} %get-tuple-element.215), channel_id=1, source_target_pairs={{240,0},{244,4},{248,8},{252,12},{0,16},{4,20},{8,24},{12,28},{16,... | collective-permute-start | bytes 1572872 | tf_op jit(solution)/shard_map/while/body/eval_jaxpr/ppermute | solution.py:22
  249.6 16.1 %collective-permute-start = (bf16[256,1024]{1,0:T(8,128)(2,1)S(1)}, bf16[256,1024]{1,0:T(8,128)(2,1)S(1)}, u32[]{:S(2)}, u32[]{:S(2)}) collective-permute-start(bf16[256,1024]{1,0:T(8,128)(2,1)S(1)} %get-tuple-element.215), channel_id=1, source_target_pairs={{240,0},{244,4},{248,8},{252,12},{0,16},{4,20},{8,24},{12,28},{16,... | collective-permute-start | bytes 1572872 | tf_op jit(solution)/shard_map/while/body/eval_jaxpr/ppermute | solution.py:22
  267.0 15.2 %collective-permute-start = (bf16[256,1024]{1,0:T(8,128)(2,1)S(1)}, bf16[256,1024]{1,0:T(8,128)(2,1)S(1)}, u32[]{:S(2)}, u32[]{:S(2)}) collective-permute-start(bf16[256,1024]{1,0:T(8,128)(2,1)S(1)} %get-tuple-element.215), channel_id=1, source_target_pairs={{240,0},{244,4},{248,8},{252,12},{0,16},{4,20},{8,24},{12,28},{16,... | collective-permute-start | bytes 1572872 | tf_op jit(solution)/shard_map/while/body/eval_jaxpr/ppermute | solution.py:22
  283.5 14.3 %collective-permute-start = (bf16[256,1024]{1,0:T(8,128)(2,1)S(1)}, bf16[256,1024]{1,0:T(8,128)(2,1)S(1)}, u32[]{:S(2)}, u32[]{:S(2)}) collective-permute-start(bf16[256,1024]{1,0:T(8,128)(2,1)S(1)} %get-tuple-element.215), channel_id=1, source_target_pairs={{240,0},{244,4},{248,8},{252,12},{0,16},{4,20},{8,24},{12,28},{16,... | collective-permute-start | bytes 1572872 | tf_op jit(solution)/shard_map/while/body/eval_jaxpr/ppermute | solution.py:22
  299.1 11.3 %collective-permute-start = (bf16[256,1024]{1,0:T(8,128)(2,1)S(1)}, bf16[256,1024]{1,0:T(8,128)(2,1)S(1)}, u32[]{:S(2)}, u32[]{:S(2)}) collective-permute-start(bf16[256,1024]{1,0:T(8,128)(2,1)S(1)} %get-tuple-element.215), channel_id=1, source_target_pairs={{240,0},{244,4},{248,8},{252,12},{0,16},{4,20},{8,24},{12,28},{16,... | collective-permute-start | bytes 1572872 | tf_op jit(solution)/shard_map/while/body/eval_jaxpr/ppermute | solution.py:22
Sparse Core Ops, SparseCore 0:
  9.2 27.6 all-gather.1
where the time goes:
time: 319 us
  waiting for transfers between devices  243 us (76%)
  matrix products  22.4 us (7%)
  starting transfers between devices  22.2 us (7%)
  between operations  13.8 us (4%)
  local copies, waits for them, and re-layouts  11.1 us (3%)
  other arithmetic  5.64 us (2%)
    ppermute x15, waiting for transfers between devices, from_behind(): return lax.ppermute(block, axis, route)  210 us
    all_gather x1, waiting for transfers between devices, local(): lax.all_gather(samples, 'team', axis=0, tiled=True)  26 us
    ppermute x6, starting transfers between devices, shifted(): return lax.ppermute(array, axis, pairs)  22.2 us
    dot_general x16, matrix products, place_tile(): jnp.einsum('crk,pk->crp', local_pair, partner, preferred_element_type=jnp...  19.7 us
    ppermute x6, waiting for transfers between devices, shifted(): return lax.ppermute(array, axis, pairs)  6.8 us
  transfers between devices with their start and end apart: 22, of which 18 were waited for; matrix products, arithmetic and copies ran while one was open for 1% of the time, Pallas kernels for 0%

commit v1 on v0

--- a/solution.py
+++ b/solution.py
@@ -8,6 +8,15 @@
 TAPS = 8
 AVG = 32
 SPEC = 16
+
+
+def wrap_the_shelves(which_axis, slab_in):
+    return jnp.concatenate(
+        jax.lax.all_to_all(
+            jnp.stack([slab_in for _ in range(jax.lax.axis_size(which_axis))]), which_axis, 0, 0
+        ),
+        axis=0,
+    )
 
 
 def shifted(array, axis, by):
@@ -80,9 +89,7 @@
     bin_range = jnp.arange(bin_groups, dtype=jnp.int32)
     avg_range = jnp.arange(AVG, dtype=jnp.int32)
     own_channels = (bin_range[:, None] * team_size + member) * AVG + avg_range[None, :]
-    spectra = filter_bank(lax.all_gather(samples, "team", axis=0, tiled=True), own_channels[None])[
-        :, 0
-    ]
+    spectra = filter_bank(wrap_the_shelves("team", samples), own_channels[None])[:, 0]
     packed_all = apply_gains(spectra, input_gains)
     width_k = packed_all.shape[2]
     own_part = lax.dynamic_index_in_dim(packed_all, bin_slot, 0, keepdims=False)

time: 319 us -> 303 us (0.950)
  between operations: 13.8 us -> 0.45 us
  waiting for transfers between devices: 243 us -> 232 us
  starting transfers between devices: 22.2 us -> 28.2 us
    all_gather x1 -> x0, waiting for transfers between devices: 26 us -> none  [local(): lax.all_gather(samples, 'team', axis=0, tiled=True)]
    all_to_all x0 -> x1, waiting for transfers between devices: none -> 18.2 us  [wrap_the_shelves(): jax.lax.all_to_all(jnp.stack([slab_in for _ in range(jax.lax.axis_size(wh...]
    all_to_all x0 -> x1, starting transfers between devices: none -> 4.34 us  [wrap_the_shelves(): jax.lax.all_to_all(jnp.stack([slab_in for _ in range(jax.lax.axis_size(wh...]
where the time goes in v1:
time: 303 us; the launch traced here: 301 us
  waiting for transfers between devices  232 us (77%)
  starting transfers between devices  28.2 us (9%)
  matrix products  22.4 us (7%)
  local copies, waits for them, and re-layouts  12.4 us (4%)
  other arithmetic  5.67 us (2%)
    ppermute x15, waiting for transfers between devices, from_behind(): return lax.ppermute(block, axis, route)  208 us
    ppermute x6, starting transfers between devices, shifted(): return lax.ppermute(array, axis, pairs)  23.8 us
    dot_general x16, matrix products, place_tile(): jnp.einsum('crk,pk->crp', local_pair, partner, preferred_element_type=jnp...  19.7 us
    all_to_all x1, waiting for transfers between devices, wrap_the_shelves(): jax.lax.all_to_all(jnp.stack([slab_in for _ in range(jax.lax.axis_size(wh...  18.2 us
    ppermute x6, waiting for transfers between devices, shifted(): return lax.ppermute(array, axis, pairs)  6.2 us
  transfers between devices with their start and end apart: 22, of which 18 were waited for; matrix products, arithmetic and copies ran while one was open for 1% of the time, Pallas kernels for 0%

profile of v1, /device:TPU:26, one launch (start us, length us, event | category | flops | bytes accessed | tf_op | source)
XLA Modules:
  0.0 301.3 jit_solution(15333697400798107531)
XLA Ops:
  0.0 2.2 stack.8
  2.2 4.3 %all-to-all-start = ((bf16[4,16,11776]{2,1,0:T(8,128)(2,1)}), bf16[4,16,11776]{2,1,0:T(8,128)(2,1)}, u32[]{:S(2)}, u32[]{:S(2)}) async-start(bf16[4,16,11776]{2,1,0:T(8,128)(2,1)} %stack.8), calls=%async_computation | async-start | bytes 3014656 | tf_op jit(solution)/shard_map/all_to_all | solution.py:15
  7.6 1.8 fusion.26
  9.3 18.2 %all-to-all-done = bf16[4,16,11776]{2,1,0:T(8,128)(2,1)} async-done(((bf16[4,16,11776]{2,1,0:T(8,128)(2,1)}), bf16[4,16,11776]{2,1,0:T(8,128)(2,1)}, u32[]{:S(2)}, u32[]{:S(2)}) %all-to-all-start) | async-done | bytes 1507360 | tf_op jit(solution)/shard_map/all_to_all | solution.py:15
  27.5 2.7 reshape.163
  30.2 2.8 fusion.2
  33.0 2.7 fusion.11
  38.1 2.1 collective-permute-start.1
  40.2 9.8 %collective-permute-start.2 = (bf16[64,1024]{1,0:T(8,128)(2,1)S(1)}, bf16[64,1024]{1,0:T(8,128)(2,1)S(1)}, u32[]{:S(2)}, u32[]{:S(2)}) collective-permute-start(bf16[64,1024]{1,0:T(8,128)(2,1)S(1)} %bitcast.98), channel_id=1, source_target_pairs={{8,0},{12,4},{16,8},{20,12},{24,16},{28,20},{32,24},{36,28},{40,32... | collective-permute-start | bytes 393224 | tf_op jit(solution)/shard_map/ppermute | solution.py:25
  50.0 1.9 collective-permute-start.3
  51.9 6.0 %collective-permute-start.4 = (bf16[64,1024]{1,0:T(8,128)(2,1)S(1)}, bf16[64,1024]{1,0:T(8,128)(2,1)S(1)}, u32[]{:S(2)}, u32[]{:S(2)}) collective-permute-start(bf16[64,1024]{1,0:T(8,128)(2,1)S(1)} %bitcast.96), channel_id=1, source_target_pairs={{0,4},{4,8},{8,12},{12,16},{16,20},{20,24},{24,28},{28,32},{32,36}... | collective-permute-start | bytes 393224 | tf_op jit(solution)/shard_map/ppermute | solution.py:25
  58.1 2.0 collective-permute-start.5
  60.2 1.9 collective-permute-start.6
  62.4 4.2 %collective-permute-done.5 = bf16[64,1024]{1,0:T(8,128)(2,1)S(1)} collective-permute-done((bf16[64,1024]{1,0:T(8,128)(2,1)S(1)}, bf16[64,1024]{1,0:T(8,128)(2,1)S(1)}, u32[]{:S(2)}, u32[]{:S(2)}) %collective-permute-start.5) | collective-permute-done | bytes 131104 | tf_op jit(solution)/shard_map/ppermute | solution.py:25
  66.6 2.0 collective-permute-done.6
  68.9 1.0 broadcast_in_dim.44
  70.4 3.4 %copy-done = f32[2,256,4096]{2,1,0:T(8,128)} copy-done((f32[2,256,4096]{2,1,0:T(8,128)}, f32[2,256,4096]{2,1,0:T(8,128)S(1)}, u32[]{:S(2)}) %copy-start) | copy-done | bytes 8388632
  73.8 227.5 %while.17 = (s32[]{:T(128)}, bf16[256,1024]{1,0:T(8,128)(2,1)S(1)}, f32[2,256,4096]{2,1,0:T(8,128)}, bf16[2,256,1024]{2,1,0:T(8,128)(2,1)S(1)}, s32[]{:T(128)}, ...) while((s32[]{:T(128)}, bf16[256,1024]{1,0:T(8,128)(2,1)S(1)}, ...), condition=%wide.region_1.2_spmd, body=%wide.region_0.1_spmd.sunk | while | flops 268566560 | bytes 5243200 | solution.py:134
  73.8 14.9 %collective-permute-done = bf16[256,1024]{1,0:T(8,128)(2,1)S(1)} collective-permute-done((bf16[256,1024]{1,0:T(8,128)(2,1)S(1)}, bf16[256,1024]{1,0:T(8,128)(2,1)S(1)}, u32[]{:S(2)}, u32[]{:S(2)}) %collective-permute-start) | collective-permute-done | bytes 524320 | tf_op jit(solution)/shard_map/while/body/eval_jaxpr/ppermute | solution.py:31
  88.8 1.3 fusion.51
  90.1 14.0 %collective-permute-done = bf16[256,1024]{1,0:T(8,128)(2,1)S(1)} collective-permute-done((bf16[256,1024]{1,0:T(8,128)(2,1)S(1)}, bf16[256,1024]{1,0:T(8,128)(2,1)S(1)}, u32[]{:S(2)}, u32[]{:S(2)}) %collective-permute-start) | collective-permute-done | bytes 524320 | tf_op jit(solution)/shard_map/while/body/eval_jaxpr/ppermute | solution.py:31
  104.1 1.3 fusion.51
  105.4 13.1 %collective-permute-done = bf16[256,1024]{1,0:T(8,128)(2,1)S(1)} collective-permute-done((bf16[256,1024]{1,0:T(8,128)(2,1)S(1)}, bf16[256,1024]{1,0:T(8,128)(2,1)S(1)}, u32[]{:S(2)}, u32[]{:S(2)}) %collective-permute-start) | collective-permute-done | bytes 524320 | tf_op jit(solution)/shard_map/while/body/eval_jaxpr/ppermute | solution.py:31
  118.5 1.3 fusion.51
  119.8 12.2 %collective-permute-done = bf16[256,1024]{1,0:T(8,128)(2,1)S(1)} collective-permute-done((bf16[256,1024]{1,0:T(8,128)(2,1)S(1)}, bf16[256,1024]{1,0:T(8,128)(2,1)S(1)}, u32[]{:S(2)}, u32[]{:S(2)}) %collective-permute-start) | collective-permute-done | bytes 524320 | tf_op jit(solution)/shard_map/while/body/eval_jaxpr/ppermute | solution.py:31
  132.0 1.3 fusion.51
  133.3 11.3 %collective-permute-done = bf16[256,1024]{1,0:T(8,128)(2,1)S(1)} collective-permute-done((bf16[256,1024]{1,0:T(8,128)(2,1)S(1)}, bf16[256,1024]{1,0:T(8,128)(2,1)S(1)}, u32[]{:S(2)}, u32[]{:S(2)}) %collective-permute-start) | collective-permute-done | bytes 524320 | tf_op jit(solution)/shard_map/while/body/eval_jaxpr/ppermute | solution.py:31
  144.6 1.3 fusion.51
  145.9 12.2 %collective-permute-done = bf16[256,1024]{1,0:T(8,128)(2,1)S(1)} collective-permute-done((bf16[256,1024]{1,0:T(8,128)(2,1)S(1)}, bf16[256,1024]{1,0:T(8,128)(2,1)S(1)}, u32[]{:S(2)}, u32[]{:S(2)}) %collective-permute-start) | collective-permute-done | bytes 524320 | tf_op jit(solution)/shard_map/while/body/eval_jaxpr/ppermute | solution.py:31
  158.1 1.3 fusion.51
  159.4 13.3 %collective-permute-done = bf16[256,1024]{1,0:T(8,128)(2,1)S(1)} collective-permute-done((bf16[256,1024]{1,0:T(8,128)(2,1)S(1)}, bf16[256,1024]{1,0:T(8,128)(2,1)S(1)}, u32[]{:S(2)}, u32[]{:S(2)}) %collective-permute-start) | collective-permute-done | bytes 524320 | tf_op jit(solution)/shard_map/while/body/eval_jaxpr/ppermute | solution.py:31
  172.7 1.3 fusion.51
  174.0 14.3 %collective-permute-done = bf16[256,1024]{1,0:T(8,128)(2,1)S(1)} collective-permute-done((bf16[256,1024]{1,0:T(8,128)(2,1)S(1)}, bf16[256,1024]{1,0:T(8,128)(2,1)S(1)}, u32[]{:S(2)}, u32[]{:S(2)}) %collective-permute-start) | collective-permute-done | bytes 524320 | tf_op jit(solution)/shard_map/while/body/eval_jaxpr/ppermute | solution.py:31
  188.4 1.3 fusion.51
  189.7 15.4 %collective-permute-done = bf16[256,1024]{1,0:T(8,128)(2,1)S(1)} collective-permute-done((bf16[256,1024]{1,0:T(8,128)(2,1)S(1)}, bf16[256,1024]{1,0:T(8,128)(2,1)S(1)}, u32[]{:S(2)}, u32[]{:S(2)}) %collective-permute-start) | collective-permute-done | bytes 524320 | tf_op jit(solution)/shard_map/while/body/eval_jaxpr/ppermute | solution.py:31
  205.2 1.3 fusion.51
  206.4 16.6 %collective-permute-done = bf16[256,1024]{1,0:T(8,128)(2,1)S(1)} collective-permute-done((bf16[256,1024]{1,0:T(8,128)(2,1)S(1)}, bf16[256,1024]{1,0:T(8,128)(2,1)S(1)}, u32[]{:S(2)}, u32[]{:S(2)}) %collective-permute-start) | collective-permute-done | bytes 524320 | tf_op jit(solution)/shard_map/while/body/eval_jaxpr/ppermute | solution.py:31
  223.1 1.3 fusion.51
  224.3 16.1 %collective-permute-done = bf16[256,1024]{1,0:T(8,128)(2,1)S(1)} collective-permute-done((bf16[256,1024]{1,0:T(8,128)(2,1)S(1)}, bf16[256,1024]{1,0:T(8,128)(2,1)S(1)}, u32[]{:S(2)}, u32[]{:S(2)}) %collective-permute-start) | collective-permute-done | bytes 524320 | tf_op jit(solution)/shard_map/while/body/eval_jaxpr/ppermute | solution.py:31
  240.5 1.3 fusion.51
  241.7 15.2 %collective-permute-done = bf16[256,1024]{1,0:T(8,128)(2,1)S(1)} collective-permute-done((bf16[256,1024]{1,0:T(8,128)(2,1)S(1)}, bf16[256,1024]{1,0:T(8,128)(2,1)S(1)}, u32[]{:S(2)}, u32[]{:S(2)}) %collective-permute-start) | collective-permute-done | bytes 524320 | tf_op jit(solution)/shard_map/while/body/eval_jaxpr/ppermute | solution.py:31
  257.0 1.3 fusion.51
  258.3 14.3 %collective-permute-done = bf16[256,1024]{1,0:T(8,128)(2,1)S(1)} collective-permute-done((bf16[256,1024]{1,0:T(8,128)(2,1)S(1)}, bf16[256,1024]{1,0:T(8,128)(2,1)S(1)}, u32[]{:S(2)}, u32[]{:S(2)}) %collective-permute-start) | collective-permute-done | bytes 524320 | tf_op jit(solution)/shard_map/while/body/eval_jaxpr/ppermute | solution.py:31
  272.7 1.3 fusion.51
  274.0 13.4 %collective-permute-done = bf16[256,1024]{1,0:T(8,128)(2,1)S(1)} collective-permute-done((bf16[256,1024]{1,0:T(8,128)(2,1)S(1)}, bf16[256,1024]{1,0:T(8,128)(2,1)S(1)}, u32[]{:S(2)}, u32[]{:S(2)}) %collective-permute-start) | collective-permute-done | bytes 524320 | tf_op jit(solution)/shard_map/while/body/eval_jaxpr/ppermute | solution.py:31
  287.4 1.3 fusion.51
  288.7 11.3 %collective-permute-done = bf16[256,1024]{1,0:T(8,128)(2,1)S(1)} collective-permute-done((bf16[256,1024]{1,0:T(8,128)(2,1)S(1)}, bf16[256,1024]{1,0:T(8,128)(2,1)S(1)}, u32[]{:S(2)}, u32[]{:S(2)}) %collective-permute-start) | collective-permute-done | bytes 524320 | tf_op jit(solution)/shard_map/while/body/eval_jaxpr/ppermute | solution.py:31
  300.0 1.3 fusion.51
  (75 shorter events, 4.8 us)
Async XLA Ops:
  0.0 7.6 %copy-start.2 = (f32[2,64,4,32]{1,3,2,0:T(8,128)S(1)}, f32[2,64,4,32]{1,3,2,0:T(8,128)}, u32[]{:S(2)}) copy-start(f32[2,64,4,32]{1,3,2,0:T(8,128)} %param.5) | copy-start | bytes 196612
  2.2 25.3 %all-to-all-start = ((bf16[4,16,11776]{2,1,0:T(8,128)(2,1)}), bf16[4,16,11776]{2,1,0:T(8,128)(2,1)}, u32[]{:S(2)}, u32[]{:S(2)}) async-start(bf16[4,16,11776]{2,1,0:T(8,128)(2,1)} %stack.8), calls=%async_computation | async-start | bytes 3014656 | tf_op jit(solution)/shard_map/all_to_all | solution.py:15
  30.2 2.8 copy-start.1
  38.1 22.0 %collective-permute-start.1 = (bf16[64,1024]{1,0:T(8,128)(2,1)S(1)}, bf16[64,1024]{1,0:T(8,128)(2,1)S(1)}, u32[]{:S(2)}, u32[]{:S(2)}) collective-permute-start(bf16[64,1024]{1,0:T(8,128)(2,1)S(1)} %bitcast.99), channel_id=1, source_target_pairs={{12,0},{16,4},{20,8},{24,12},{28,16},{32,20},{36,24},{40,28},{44,3... | collective-permute-start | bytes 393224 | tf_op jit(solution)/shard_map/ppermute | solution.py:25
  40.2 21.9 %collective-permute-start.2 = (bf16[64,1024]{1,0:T(8,128)(2,1)S(1)}, bf16[64,1024]{1,0:T(8,128)(2,1)S(1)}, u32[]{:S(2)}, u32[]{:S(2)}) collective-permute-start(bf16[64,1024]{1,0:T(8,128)(2,1)S(1)} %bitcast.98), channel_id=1, source_target_pairs={{8,0},{12,4},{16,8},{20,12},{24,16},{28,20},{32,24},{36,28},{40,32... | collective-permute-start | bytes 393224 | tf_op jit(solution)/shard_map/ppermute | solution.py:25
  50.0 12.2 %collective-permute-start.3 = (bf16[64,1024]{1,0:T(8,128)(2,1)S(1)}, bf16[64,1024]{1,0:T(8,128)(2,1)S(1)}, u32[]{:S(2)}, u32[]{:S(2)}) collective-permute-start(bf16[64,1024]{1,0:T(8,128)(2,1)S(1)} %bitcast.97), channel_id=1, source_target_pairs={{4,0},{8,4},{12,8},{16,12},{20,16},{24,20},{28,24},{32,28},{36,32}... | collective-permute-start | bytes 393224 | tf_op jit(solution)/shard_map/ppermute | solution.py:25
  51.9 10.4 %collective-permute-start.4 = (bf16[64,1024]{1,0:T(8,128)(2,1)S(1)}, bf16[64,1024]{1,0:T(8,128)(2,1)S(1)}, u32[]{:S(2)}, u32[]{:S(2)}) collective-permute-start(bf16[64,1024]{1,0:T(8,128)(2,1)S(1)} %bitcast.96), channel_id=1, source_target_pairs={{0,4},{4,8},{8,12},{12,16},{16,20},{20,24},{24,28},{28,32},{32,36}... | collective-permute-start | bytes 393224 | tf_op jit(solution)/shard_map/ppermute | solution.py:25
  58.1 8.5 %collective-permute-start.5 = (bf16[64,1024]{1,0:T(8,128)(2,1)S(1)}, bf16[64,1024]{1,0:T(8,128)(2,1)S(1)}, u32[]{:S(2)}, u32[]{:S(2)}) collective-permute-start(bf16[64,1024]{1,0:T(8,128)(2,1)S(1)} %bitcast.95), channel_id=1, source_target_pairs={{0,8},{4,12},{8,16},{12,20},{16,24},{20,28},{24,32},{28,36},{32,40... | collective-permute-start | bytes 393224 | tf_op jit(solution)/shard_map/ppermute | solution.py:25
  60.2 8.4 %collective-permute-start.6 = (bf16[64,1024]{1,0:T(8,128)(2,1)S(1)}, bf16[64,1024]{1,0:T(8,128)(2,1)S(1)}, u32[]{:S(2)}, u32[]{:S(2)}) collective-permute-start(bf16[64,1024]{1,0:T(8,128)(2,1)S(1)} %bitcast.94), channel_id=1, source_target_pairs={{0,12},{4,16},{8,20},{12,24},{16,28},{20,32},{24,36},{28,40},{32,4... | collective-permute-start | bytes 393224 | tf_op jit(solution)/shard_map/ppermute | solution.py:25
  70.4 3.4 %copy-start = (f32[2,256,4096]{2,1,0:T(8,128)}, f32[2,256,4096]{2,1,0:T(8,128)S(1)}, u32[]{:S(2)}) copy-start(f32[2,256,4096]{2,1,0:T(8,128)S(1)} %fusion.14) | copy-start | bytes 25165828
  73.8 14.9 %collective-permute-start = (bf16[256,1024]{1,0:T(8,128)(2,1)S(1)}, bf16[256,1024]{1,0:T(8,128)(2,1)S(1)}, u32[]{:S(2)}, u32[]{:S(2)}) collective-permute-start(bf16[256,1024]{1,0:T(8,128)(2,1)S(1)} %get-tuple-element.215), channel_id=1, source_target_pairs={{240,0},{244,4},{248,8},{252,12},{0,16},{4,20},{8,24},{12,28},{16,... | collective-permute-start | bytes 1572872 | tf_op jit(solution)/shard_map/while/body/eval_jaxpr/ppermute | solution.py:31
  90.1 14.0 %collective-permute-start = (bf16[256,1024]{1,0:T(8,128)(2,1)S(1)}, bf16[256,1024]{1,0:T(8,128)(2,1)S(1)}, u32[]{:S(2)}, u32[]{:S(2)}) collective-permute-start(bf16[256,1024]{1,0:T(8,128)(2,1)S(1)} %get-tuple-element.215), channel_id=1, source_target_pairs={{240,0},{244,4},{248,8},{252,12},{0,16},{4,20},{8,24},{12,28},{16,... | collective-permute-start | bytes 1572872 | tf_op jit(solution)/shard_map/while/body/eval_jaxpr/ppermute | solution.py:31
  105.4 13.1 %collective-permute-start = (bf16[256,1024]{1,0:T(8,128)(2,1)S(1)}, bf16[256,1024]{1,0:T(8,128)(2,1)S(1)}, u32[]{:S(2)}, u32[]{:S(2)}) collective-permute-start(bf16[256,1024]{1,0:T(8,128)(2,1)S(1)} %get-tuple-element.215), channel_id=1, source_target_pairs={{240,0},{244,4},{248,8},{252,12},{0,16},{4,20},{8,24},{12,28},{16,... | collective-permute-start | bytes 1572872 | tf_op jit(solution)/shard_map/while/body/eval_jaxpr/ppermute | solution.py:31
  119.8 12.2 %collective-permute-start = (bf16[256,1024]{1,0:T(8,128)(2,1)S(1)}, bf16[256,1024]{1,0:T(8,128)(2,1)S(1)}, u32[]{:S(2)}, u32[]{:S(2)}) collective-permute-start(bf16[256,1024]{1,0:T(8,128)(2,1)S(1)} %get-tuple-element.215), channel_id=1, source_target_pairs={{240,0},{244,4},{248,8},{252,12},{0,16},{4,20},{8,24},{12,28},{16,... | collective-permute-start | bytes 1572872 | tf_op jit(solution)/shard_map/while/body/eval_jaxpr/ppermute | solution.py:31
  133.3 11.3 %collective-permute-start = (bf16[256,1024]{1,0:T(8,128)(2,1)S(1)}, bf16[256,1024]{1,0:T(8,128)(2,1)S(1)}, u32[]{:S(2)}, u32[]{:S(2)}) collective-permute-start(bf16[256,1024]{1,0:T(8,128)(2,1)S(1)} %get-tuple-element.215), channel_id=1, source_target_pairs={{240,0},{244,4},{248,8},{252,12},{0,16},{4,20},{8,24},{12,28},{16,... | collective-permute-start | bytes 1572872 | tf_op jit(solution)/shard_map/while/body/eval_jaxpr/ppermute | solution.py:31
  145.9 12.2 %collective-permute-start = (bf16[256,1024]{1,0:T(8,128)(2,1)S(1)}, bf16[256,1024]{1,0:T(8,128)(2,1)S(1)}, u32[]{:S(2)}, u32[]{:S(2)}) collective-permute-start(bf16[256,1024]{1,0:T(8,128)(2,1)S(1)} %get-tuple-element.215), channel_id=1, source_target_pairs={{240,0},{244,4},{248,8},{252,12},{0,16},{4,20},{8,24},{12,28},{16,... | collective-permute-start | bytes 1572872 | tf_op jit(solution)/shard_map/while/body/eval_jaxpr/ppermute | solution.py:31
  159.4 13.3 %collective-permute-start = (bf16[256,1024]{1,0:T(8,128)(2,1)S(1)}, bf16[256,1024]{1,0:T(8,128)(2,1)S(1)}, u32[]{:S(2)}, u32[]{:S(2)}) collective-permute-start(bf16[256,1024]{1,0:T(8,128)(2,1)S(1)} %get-tuple-element.215), channel_id=1, source_target_pairs={{240,0},{244,4},{248,8},{252,12},{0,16},{4,20},{8,24},{12,28},{16,... | collective-permute-start | bytes 1572872 | tf_op jit(solution)/shard_map/while/body/eval_jaxpr/ppermute | solution.py:31
  174.0 14.4 %collective-permute-start = (bf16[256,1024]{1,0:T(8,128)(2,1)S(1)}, bf16[256,1024]{1,0:T(8,128)(2,1)S(1)}, u32[]{:S(2)}, u32[]{:S(2)}) collective-permute-start(bf16[256,1024]{1,0:T(8,128)(2,1)S(1)} %get-tuple-element.215), channel_id=1, source_target_pairs={{240,0},{244,4},{248,8},{252,12},{0,16},{4,20},{8,24},{12,28},{16,... | collective-permute-start | bytes 1572872 | tf_op jit(solution)/shard_map/while/body/eval_jaxpr/ppermute | solution.py:31
  189.7 15.4 %collective-permute-start = (bf16[256,1024]{1,0:T(8,128)(2,1)S(1)}, bf16[256,1024]{1,0:T(8,128)(2,1)S(1)}, u32[]{:S(2)}, u32[]{:S(2)}) collective-permute-start(bf16[256,1024]{1,0:T(8,128)(2,1)S(1)} %get-tuple-element.215), channel_id=1, source_target_pairs={{240,0},{244,4},{248,8},{252,12},{0,16},{4,20},{8,24},{12,28},{16,... | collective-permute-start | bytes 1572872 | tf_op jit(solution)/shard_map/while/body/eval_jaxpr/ppermute | solution.py:31
  206.4 16.6 %collective-permute-start = (bf16[256,1024]{1,0:T(8,128)(2,1)S(1)}, bf16[256,1024]{1,0:T(8,128)(2,1)S(1)}, u32[]{:S(2)}, u32[]{:S(2)}) collective-permute-start(bf16[256,1024]{1,0:T(8,128)(2,1)S(1)} %get-tuple-element.215), channel_id=1, source_target_pairs={{240,0},{244,4},{248,8},{252,12},{0,16},{4,20},{8,24},{12,28},{16,... | collective-permute-start | bytes 1572872 | tf_op jit(solution)/shard_map/while/body/eval_jaxpr/ppermute | solution.py:31
  224.3 16.1 %collective-permute-start = (bf16[256,1024]{1,0:T(8,128)(2,1)S(1)}, bf16[256,1024]{1,0:T(8,128)(2,1)S(1)}, u32[]{:S(2)}, u32[]{:S(2)}) collective-permute-start(bf16[256,1024]{1,0:T(8,128)(2,1)S(1)} %get-tuple-element.215), channel_id=1, source_target_pairs={{240,0},{244,4},{248,8},{252,12},{0,16},{4,20},{8,24},{12,28},{16,... | collective-permute-start | bytes 1572872 | tf_op jit(solution)/shard_map/while/body/eval_jaxpr/ppermute | solution.py:31
  241.7 15.3 %collective-permute-start = (bf16[256,1024]{1,0:T(8,128)(2,1)S(1)}, bf16[256,1024]{1,0:T(8,128)(2,1)S(1)}, u32[]{:S(2)}, u32[]{:S(2)}) collective-permute-start(bf16[256,1024]{1,0:T(8,128)(2,1)S(1)} %get-tuple-element.215), channel_id=1, source_target_pairs={{240,0},{244,4},{248,8},{252,12},{0,16},{4,20},{8,24},{12,28},{16,... | collective-permute-start | bytes 1572872 | tf_op jit(solution)/shard_map/while/body/eval_jaxpr/ppermute | solution.py:31
  258.3 14.3 %collective-permute-start = (bf16[256,1024]{1,0:T(8,128)(2,1)S(1)}, bf16[256,1024]{1,0:T(8,128)(2,1)S(1)}, u32[]{:S(2)}, u32[]{:S(2)}) collective-permute-start(bf16[256,1024]{1,0:T(8,128)(2,1)S(1)} %get-tuple-element.215), channel_id=1, source_target_pairs={{240,0},{244,4},{248,8},{252,12},{0,16},{4,20},{8,24},{12,28},{16,... | collective-permute-start | bytes 1572872 | tf_op jit(solution)/shard_map/while/body/eval_jaxpr/ppermute | solution.py:31
  274.0 13.4 %collective-permute-start = (bf16[256,1024]{1,0:T(8,128)(2,1)S(1)}, bf16[256,1024]{1,0:T(8,128)(2,1)S(1)}, u32[]{:S(2)}, u32[]{:S(2)}) collective-permute-start(bf16[256,1024]{1,0:T(8,128)(2,1)S(1)} %get-tuple-element.215), channel_id=1, source_target_pairs={{240,0},{244,4},{248,8},{252,12},{0,16},{4,20},{8,24},{12,28},{16,... | collective-permute-start | bytes 1572872 | tf_op jit(solution)/shard_map/while/body/eval_jaxpr/ppermute | solution.py:31
  288.7 11.3 %collective-permute-start = (bf16[256,1024]{1,0:T(8,128)(2,1)S(1)}, bf16[256,1024]{1,0:T(8,128)(2,1)S(1)}, u32[]{:S(2)}, u32[]{:S(2)}) collective-permute-start(bf16[256,1024]{1,0:T(8,128)(2,1)S(1)} %get-tuple-element.215), channel_id=1, source_target_pairs={{240,0},{244,4},{248,8},{252,12},{0,16},{4,20},{8,24},{12,28},{16,... | collective-permute-start | bytes 1572872 | tf_op jit(solution)/shard_map/while/body/eval_jaxpr/ppermute | solution.py:31
